TPU v7x, 256 devices: a whole 4x4x8 slice. The times are simulated.
256 devices in a mesh: lat: 8 (over y_lo, x), lon: 32 (over z, y_hi, core).
Axes of the slice: x: 4, y: 4 (y_hi: 2, y_lo: 2; y = y_hi * 2 + y_lo), z: 8, core: 2. Of those that a mesh axis runs over, the one named last changes fastest.
Arguments:
- background: bfloat16 [69, 64, 32, 8, 128], P(None, None, 'lon', 'lat'), may hold values from -6 to 6
- obs_ens: bfloat16 [4, 8, 32, 32, 64, 128], P(None, 'lat', 'lon'), may hold values from -6 to 6
- obs_value: bfloat16 [4, 8, 32, 32, 128], P(None, 'lat', 'lon'), may hold values from -10 to 10
- obs_prec: bfloat16 [4, 8, 32, 32, 128], P(None, 'lat', 'lon'), may hold values from 0.019897461 to 0.5
- obs_count: int32 [4, 8, 32], P(None, 'lat', 'lon'), may hold values from 32 to 128, as said below
- slot_owner: int32 [4], replicated, may hold values from 0 to 31
- region_slots: int32 [64, 128, 2], P('lon', 'lat'), may hold values from 0 to 3, as said below
Outputs:
- analysis: bfloat16 [69, 64, 32, 8, 128], P(None, None, 'lon', 'lat')
Inputs may be any that keep to these rules, and one draw needn't show every extreme that they name: The first obs_count entries of a patch's block in a slot are live; the largest value 128 occurs in every draw. `region_slots`: the 2 slots of a region are distinct.
All inputs are finite; a program needn't handle non-finite values.
Results may differ from a plain program's by a relative error of at most 0.0095.
Values may be sent and summed in bfloat16 or wider, within the bound.
No kernel may reach another device: no remote copies, remote signals or barrier semaphores. Data moves between devices by JAX's collectives and lax.ppermute only.
A program may use at most 64 MiB of HBM per device.

v0:
```python
import functools
import math

import jax
import jax.numpy as jnp
from jax import lax
from jax.experimental import pallas as pl
from jax.experimental.pallas import tpu as pltpu
from jax.sharding import PartitionSpec as P

MEMBERS = 64
FIELDS = 69
CELLS_LAT = 32
CELLS_LON = 4
PATCH_CELLS = 128
SLOTS = 4
OBS_BLOCK = 128
NEWTON_STEPS = 3
LON_PAIRS = 2
LAT_PAIRS = 16
PAIRS = ((0, 1), (0, 2), (0, 3), (1, 2), (1, 3), (2, 3))
ROWS = 66
PAIR_ROWS = 192
COEF_ROWS = 16
MSG_ROWS = PAIR_ROWS + MEMBERS + COEF_ROWS
CHIPS = 16
N_LAT = 8
SAME_CORE = [[j for j in range(32) if j % 2 == core] for core in range(2)]


def lon_weight(column, region):
    own = column >> 1
    outer = own + jnp.where((column & 1) == 1, 1, -1)
    return jnp.where(own == region, 0.75, jnp.where(outer == region, 0.25, 0.0))


def lat_weight(row, region):
    own = row >> 1
    outer = own + jnp.where((row & 1) == 1, 1, -1)
    return jnp.where(own == region, 0.75, jnp.where(outer == region, 0.25, 0.0))


def cell_lanes(rows):
    lane = lax.broadcasted_iota(jnp.int32, (rows, PATCH_CELLS), 1)
    return lane >> 5, lane & (CELLS_LAT - 1)


SMEM = pl.BlockSpec(memory_space=pltpu.SMEM)
VMEM = pl.BlockSpec(memory_space=pltpu.VMEM)
MIB = 1024 * 1024


def halves(array):
    high = array.astype(jnp.bfloat16)
    return high, (array - high.astype(jnp.float32)).astype(jnp.bfloat16)


def mm(left, right):
    def dot(x, y):
        return lax.dot_general(
            x, y, (((1,), (0,)), ((), ())), preferred_element_type=jnp.float32
        )

    left_high, left_low = halves(left)
    right_high, right_low = halves(right)
    return dot(left_high, right_high) + (dot(left_high, right_low) + dot(left_low, right_high))


def slot_ranks(owner_ref):
    owners = [owner_ref[s] for s in range(SLOTS)]
    ranks = []
    for s in range(SLOTS):
        rank = jnp.int32(0)
        for earlier in range(s):
            rank = rank + jnp.where((owners[earlier] >> 1) == (owners[s] >> 1), 1, 0)
        ranks.append(rank)
    return owners, ranks


def chosen_slot(owners, ranks, chip, q):
    slot = jnp.int32(0)
    owner = jnp.int32(0)
    for s in range(SLOTS):
        match = jnp.logical_and((owners[s] >> 1) == chip, ranks[s] == q)
        slot = jnp.where(match, s, slot)
        owner = jnp.where(match, owners[s], owner)
    return slot, owner


def split_kernel(
    places, owner_ref, ens_ref, value_ref, prec_ref, send_ref, keep_ref, held_ref, info_ref, index_ref,
    rows_ref, small_ref, small_sems, sems,
):
    f32 = jnp.float32
    me = lax.axis_index("lon")
    core = me & 1
    owners, ranks = slot_ranks(owner_ref)
    chosen = [chosen_slot(owners, ranks, me >> 1, q) for q in places]
    slots = [slot for slot, _ in chosen]
    for q, (_, owner) in enumerate(chosen):
        held_ref[q] = jnp.full((COEF_ROWS, OBS_BLOCK), jnp.where((owner & 1) == core, 1.0, 0.0), f32)
    most = ranks[0]
    for s in range(1, SLOTS):
        most = jnp.maximum(most, ranks[s])
    index_ref[...] = jnp.full((8, OBS_BLOCK), jnp.minimum(most, 2), jnp.int32)
    for s in range(SLOTS):
        info_ref[s : s + 1, :] = jnp.full((1, OBS_BLOCK), (owners[s] >> 1).astype(f32), f32)
        info_ref[SLOTS + s : SLOTS + s + 1, :] = jnp.full((1, OBS_BLOCK), ranks[s].astype(f32), f32)
    targets = ((send_ref, 1 - core), (keep_ref, core))
    copies = []
    smalls = []
    for q in range(len(places)):
        for k, ref in enumerate((value_ref, prec_ref)):
            copy = pltpu.make_async_copy(
                ref.at[slots[q]], small_ref.at[2 * q + k], small_sems.at[2 * q + k]
            )
            copy.start()
            smalls.append(copy)
        for k, (ref, side) in enumerate(targets):
            copy = pltpu.make_async_copy(
                ens_ref.at[slots[q], :, side], ref.at[:, q, pl.ds(0, MEMBERS)], sems.at[2 * q + k]
            )
            copy.start()
            copies.append(copy)
    for copy in smalls:
        copy.wait()
    for q in range(len(places)):
        rows_ref[0] = small_ref[2 * q].astype(f32)
        rows_ref[1] = small_ref[2 * q + 1].astype(f32)
        for ref, side in targets:
            value = rows_ref[0, pl.ds(side, CHIPS, stride=2), :]
            prec = rows_ref[1, pl.ds(side, CHIPS, stride=2), :]
            for i in range(CHIPS):
                both = jnp.concatenate([value[i : i + 1], prec[i : i + 1]], axis=0)
                ref[i, q, MEMBERS:ROWS, :] = both.astype(jnp.bfloat16)
    for copy in copies:
        copy.wait()


def split_of(places, slot_owner, obs_ens, obs_value, obs_prec):
    count = len(places)
    shape = jax.ShapeDtypeStruct((CHIPS, count, ROWS, OBS_BLOCK), jnp.bfloat16)
    return pl.pallas_call(
        functools.partial(split_kernel, places),
        out_shape=(
            shape,
            shape,
            jax.ShapeDtypeStruct((count, COEF_ROWS, OBS_BLOCK), jnp.float32),
            jax.ShapeDtypeStruct((2 * SLOTS, OBS_BLOCK), jnp.float32),
            jax.ShapeDtypeStruct((8, OBS_BLOCK), jnp.int32),
        ),
        in_specs=[SMEM] + [pl.BlockSpec(memory_space=pl.ANY)] * 3,
        out_specs=(VMEM,) * 5,
        scratch_shapes=[
            pltpu.VMEM((2, 2 * CHIPS, OBS_BLOCK), jnp.float32),
            pltpu.VMEM((2 * count, 2 * CHIPS, OBS_BLOCK), jnp.bfloat16),
            pltpu.SemaphoreType.DMA((2 * count,)),
            pltpu.SemaphoreType.DMA((2 * count,)),
        ],
        compiler_params=pltpu.CompilerParams(vmem_limit_bytes=16 * MIB),
        name="split",
    )(
        slot_owner,
        obs_ens.reshape(SLOTS, CHIPS, 2, MEMBERS, OBS_BLOCK),
        obs_value.reshape(SLOTS, 2 * CHIPS, OBS_BLOCK),
        obs_prec.reshape(SLOTS, 2 * CHIPS, OBS_BLOCK),
    )


def blend(held, keep, got):
    mine = held.astype(jnp.bfloat16)
    other = (1.0 - held).astype(jnp.bfloat16)
    return keep * mine + got * other


def merge_kernel(held_ref, keep_ref, got_ref, out_ref):
    for q in range(held_ref.shape[0]):
        out_ref[:, q] = blend(held_ref[q, 0:1, :], keep_ref[:, q], got_ref[:, q])


def append_kernel(both_ref, held_ref, keep_ref, got_ref, out_ref):
    out_ref[:, 0] = both_ref[:, 0]
    for q in range(held_ref.shape[0]):
        out_ref[:, 1 + q] = blend(held_ref[q, 0:1, :], keep_ref[:, q], got_ref[:, q])


def merge_of(held, keep, got, both=None):
    count = keep.shape[1]
    operands = (held, keep, got)
    if both is not None:
        count = count + 1
        operands = (both,) + operands
    return pl.pallas_call(
        merge_kernel if both is None else append_kernel,
        out_shape=jax.ShapeDtypeStruct((CHIPS, count, ROWS, OBS_BLOCK), keep.dtype),
        in_specs=[VMEM] * len(operands),
        out_specs=VMEM,
        compiler_params=pltpu.CompilerParams(vmem_limit_bytes=16 * MIB),
        name="merge",
    )(*operands)


def entry(row, lane):
    at = lax.broadcasted_iota(jnp.int32, row.shape, 1)
    return jnp.sum(jnp.where(at == lane, row.astype(jnp.float32), 0.0), axis=1, keepdims=True)


def pair_ids(ids_ref, a):
    one = ids_ref[a, 0:1, :]
    two = ids_ref[a, 1:2, :]
    low = jnp.minimum(one, two)
    high = jnp.maximum(one, two)
    return ((low * (7 - low)) >> 1) + (high - low - 1)


def transform_kernel(
    depth, info_ref, count_ref, ids_ref, block_ref, core_ref, swap_ref, edge_a_ref, edge_b_ref, coef_ref
):
    f32 = jnp.float32
    bf16 = jnp.bfloat16
    members = MEMBERS
    lat_par = lax.axis_index("lat") & 1
    even = (lax.axis_index("lon") & 1) == 0
    row_id = lax.broadcasted_iota(jnp.int32, (members, members), 0)
    col_id = lax.broadcasted_iota(jnp.int32, (members, members), 1)
    identity = jnp.where(row_id == col_id, 1.0, 0.0).astype(f32)
    position = lax.broadcasted_iota(jnp.int32, (1, OBS_BLOCK), 1).astype(f32)
    grams = []
    projs = []
    traces = []
    for slot in range(SLOTS):
        place = info_ref[slot : slot + 1, :] * depth + info_ref[SLOTS + slot : SLOTS + slot + 1, :]
        block = None
        for k in range(CHIPS * depth):
            here = jnp.where(place == k, 1.0, 0.0).astype(bf16)
            part = block_ref[k] * here
            block = part if block is None else block + part
        block = block.astype(f32)
        ens = block[:members]
        value = block[members : members + 1]
        prec = block[members + 1 : members + 2]
        obs_mean = jnp.sum(ens, axis=0, keepdims=True) * (1.0 / members)
        pert = (ens - obs_mean).astype(bf16)
        weight = jnp.where(position < entry(count_ref[...], slot), prec, 0.0)
        weighted = (pert.astype(f32) * weight).astype(bf16)
        diagonal = jnp.sum(weighted.astype(f32) * pert.astype(f32), axis=0, keepdims=True)
        traces.append(jnp.sum(diagonal, axis=1, keepdims=True))
        high, low = halves(value - obs_mean)
        rows = [jnp.broadcast_to(x, (COEF_ROWS, OBS_BLOCK)) for x in (high, low)]
        product = lax.dot_general(
            jnp.concatenate([pert] + rows, axis=0),
            weighted,
            (((1,), (1,)), ((), ())),
            preferred_element_type=f32,
        )
        grams.append(product[:members])
        projs.append(product[members : members + 8] + product[members + COEF_ROWS : members + COEF_ROWS + 8])
    iterates = []
    inverses = []
    scalings = []
    for first, second in PAIRS:
        matrix = grams[first] + grams[second] + (members - 1.0) * identity
        scaling = (traces[first] + traces[second]) * (1.0 / members) + (members - 1.0)
        scalings.append(scaling)
        iterate = matrix * (1.0 / scaling)
        iterates.append(iterate)
        inverses.append(1.5 * identity - 0.5 * iterate)
    sums = [projs[first] + projs[second] for first, second in PAIRS]
    iterates = [mm(x, y) for x, y in zip(iterates, inverses)]
    for step in range(1, NEWTON_STEPS):
        factors = [1.5 * identity - 0.5 * mm(y, x) for x, y in zip(iterates, inverses)]
        if step < NEWTON_STEPS - 1:
            both = [mm(jnp.concatenate([x, y], axis=0), f) for x, y, f in zip(iterates, inverses, factors)]
            iterates = [z[:members] for z in both]
            inverses = [z[members:] for z in both]
        else:
            sums = [mm(p, y) for p, y in zip(sums, inverses)]
            both = [mm(jnp.concatenate([y, p], axis=0), f) for y, p, f in zip(inverses, sums, factors)]
            inverses = [z[:members] for z in both]
            sums = [mm(z[members:], z[:members]) for z in both]
    turned = []
    for pair in range(len(PAIRS)):
        scale = 1.0 / scalings[pair]
        root = math.sqrt(members - 1.0) * jnp.sqrt(scale)
        turned.append(inverses[pair] * root + sums[pair][0:1] * scale)
        lanes = slice(pair % 2 * members, (pair % 2 + 1) * members)
        rows = pl.ds(pair // 2 * members, members)
        core_ref[rows, lanes] = turned[pair].astype(bf16)
        swap_ref[rows, lanes] = turned[pair].astype(bf16)
    ids = [pair_ids(ids_ref, a) for a in range(LON_PAIRS)]
    for which, ref in enumerate((edge_a_ref, edge_b_ref)):
        row = jnp.where(lat_par == which, LAT_PAIRS - 1, 0)
        chosen = []
        for a in range(LON_PAIRS):
            edge = entry(ids[a], row)
            one = turned[0]
            for pair in range(1, len(PAIRS)):
                one = jnp.where(edge == pair, turned[pair], one)
            chosen.append(one)
            ref[:, a * members : (a + 1) * members] = one.astype(bf16)
        lanes = slice(which * members, (which + 1) * members)
        rows = pl.ds(PAIR_ROWS, members)
        core_ref[rows, lanes] = jnp.where(even, chosen[1], chosen[0]).astype(bf16)
        swap_ref[rows, lanes] = jnp.where(even, chosen[0], chosen[1]).astype(bf16)
    tapers = jnp.zeros((COEF_ROWS, 2 * PATCH_CELLS), f32)
    pair_id = lax.broadcasted_iota(jnp.int32, (COEF_ROWS, LAT_PAIRS), 0)
    col, row = cell_lanes(LAT_PAIRS)
    lat_w = lat_weight(row, lax.broadcasted_iota(jnp.int32, (LAT_PAIRS, PATCH_CELLS), 0))
    for a in range(LON_PAIRS):
        hot = jnp.where(pair_id == ids[a], 1.0, 0.0).astype(bf16)
        outer = 0 if a == LON_PAIRS - 1 else CELLS_LON - 1
        table = jnp.concatenate(
            [lat_w * lon_weight(col, a), lat_w * jnp.where(col == outer, 0.25, 0.0)], axis=1
        )
        tapers = tapers + lax.dot_general(
            hot, table.astype(bf16), (((1,), (0,)), ((), ())), preferred_element_type=f32
        )
    coef_ref[...] = tapers[:, :PATCH_CELLS].astype(bf16)
    next_taper = tapers[:, PATCH_CELLS:].astype(bf16)
    core_ref[PAIR_ROWS + members :, :] = next_taper
    swap_ref[PAIR_ROWS + members :, :] = next_taper


def transforms_of(depth, info, counts, region_slots, blocks):
    bf16 = jnp.bfloat16
    wide = jax.ShapeDtypeStruct((MEMBERS, 2 * MEMBERS), bf16)
    coef = jax.ShapeDtypeStruct((COEF_ROWS, PATCH_CELLS), bf16)
    message = jax.ShapeDtypeStruct((MSG_ROWS, 2 * MEMBERS), bf16)
    return pl.pallas_call(
        functools.partial(transform_kernel, depth),
        out_shape=(message, message, wide, wide, coef),
        in_specs=[VMEM] * 4,
        out_specs=(VMEM,) * 5,
        compiler_params=pltpu.CompilerParams(vmem_limit_bytes=16 * MIB),
        name="transforms",
    )(info, counts.reshape(1, SLOTS), region_slots, blocks)


def pack_kernel(edge_a_ref, edge_b_ref, core_ref, swap_ref, out_a_ref, out_b_ref):
    f32 = jnp.float32
    even = (lax.axis_index("lon") & 1) == 0
    first = lax.broadcasted_iota(jnp.int32, (MEMBERS, 2 * MEMBERS), 1) < MEMBERS
    rows = pl.ds(PAIR_ROWS, MEMBERS)
    core = core_ref[rows, :].astype(f32)
    swap = swap_ref[rows, :].astype(f32)
    before = jnp.where(even, swap, core)
    after = jnp.where(even, core, swap)
    out_a_ref[0:MEMBERS] = edge_a_ref[...]
    out_b_ref[0:MEMBERS] = edge_b_ref[...]
    out_a_ref[MEMBERS:] = jnp.where(first, before, pltpu.roll(after, MEMBERS, 1)).astype(jnp.bfloat16)
    out_b_ref[MEMBERS:] = jnp.where(first, pltpu.roll(before, MEMBERS, 1), after).astype(jnp.bfloat16)


def pack_of(edge_a, edge_b, from_core, from_swap):
    shape = jax.ShapeDtypeStruct((2 * MEMBERS, 2 * MEMBERS), jnp.bfloat16)
    return pl.pallas_call(
        pack_kernel,
        out_shape=(shape, shape),
        in_specs=[VMEM] * 4,
        out_specs=(VMEM, VMEM),
        compiler_params=pltpu.CompilerParams(vmem_limit_bytes=4 * MIB),
        name="pack",
    )(edge_a, edge_b, from_core, from_swap)


def spread(row, width):
    tile = jnp.broadcast_to(row, (COEF_ROWS, PATCH_CELLS))
    return jnp.concatenate([tile] * (width // PATCH_CELLS), axis=1)


def weighted_product(left_ref, weight_ref, count, perts):
    width = perts.shape[1]
    total = None
    for first in range(0, count, 4):
        parts = []
        for k in range(first, min(first + 4, count)):
            weight = weight_ref[k, :, 0:width]
            parts.append(perts * jnp.concatenate([weight] * (MEMBERS // COEF_ROWS), axis=0))
        part = lax.dot_general(
            left_ref[:, first * MEMBERS : min(first + 4, count) * MEMBERS],
            jnp.concatenate(parts, axis=0),
            (((1,), (0,)), ((), ())),
            preferred_element_type=jnp.float32,
        )
        total = part if total is None else total + part
    return total


OWN_TERMS = 6
LAT_TERMS = 8
SIDE_TERMS = 12
CHUNK = 16
HALF = (FIELDS + 1) // 2
LAT_GROUP = 16
LAT_TILES = (FIELDS + LAT_GROUP - 1) // LAT_GROUP


def side_lanes():
    lane = lax.broadcasted_iota(jnp.int32, (MEMBERS, PATCH_CELLS), 1)
    return jnp.logical_or(lane < CELLS_LAT, lane >= PATCH_CELLS - CELLS_LAT)


def lat_lanes(field):
    lane = lax.broadcasted_iota(jnp.int32, (MEMBERS, PATCH_CELLS), 1)
    at = (lane - 2 * (field % LAT_GROUP)) & (CELLS_LAT - 1)
    return jnp.logical_or(at == 0, at == CELLS_LAT - 1)


def own_kernel(
    pair_ref, coef_ref, back_ref, sum_ref, edge_ref, rows_ref, left_ref, weight_ref
):
    f32 = jnp.float32
    bf16 = jnp.bfloat16
    for tile in range(3):
        left_ref[:, tile * 128 : (tile + 1) * 128] = pair_ref[tile * MEMBERS : (tile + 1) * MEMBERS, :]
    coefs = coef_ref[...].astype(f32)
    for k in range(OWN_TERMS):
        weight_ref[k] = spread(coefs[k : k + 1], 2 * PATCH_CELLS).astype(bf16)
    outer = side_lanes()

    def pair(first, base, count, rows):
        perts = []
        means = []
        for f in range(count):
            state = back_ref[first + f].astype(f32)
            mean = jnp.sum(state, axis=0, keepdims=True) * (1.0 / MEMBERS)
            means.append(mean)
            perts.append((state - mean).astype(bf16))
        wide = [p.astype(f32) for p in perts]
        inner = pltpu.roll(wide[1], PATCH_CELLS // 2, 1) if count == 2 else 0.0
        edge_ref[first // 2] = jnp.where(outer, wide[0], inner).astype(bf16)
        for f in range(count):
            shift = 2 * ((base + f) % LAT_GROUP)
            moved = pltpu.roll(wide[f], shift, 1) if shift else wide[f]
            rows = jnp.where(lat_lanes(base + f), moved, rows)
        both = jnp.concatenate(perts, axis=1) if count == 2 else perts[0]
        total = weighted_product(left_ref, weight_ref, OWN_TERMS, both)
        for f in range(count):
            sum_ref[first + f] = total[:, f * PATCH_CELLS : (f + 1) * PATCH_CELLS] + means[f]
        return rows

    for tile in range(LAT_TILES):
        rows = jnp.zeros((MEMBERS, PATCH_CELLS), f32)
        last = min((tile + 1) * LAT_GROUP, FIELDS)
        for first in range(tile * LAT_GROUP, last, 2):
            rows = pair(first, first, min(2, last - first), rows)
        rows_ref[tile] = rows.astype(bf16)


def own_part(message, coefs, background):
    def tiles(count, kind):
        return jax.ShapeDtypeStruct((count, MEMBERS, PATCH_CELLS), kind)

    return pl.pallas_call(
        own_kernel,
        out_shape=(
            tiles(FIELDS, jnp.float32),
            tiles(HALF, jnp.bfloat16),
            tiles(LAT_TILES, jnp.bfloat16),
        ),
        in_specs=[VMEM] * 3,
        out_specs=(VMEM,) * 3,
        scratch_shapes=[
            pltpu.VMEM((MEMBERS, OWN_TERMS * MEMBERS), jnp.bfloat16),
            pltpu.VMEM((OWN_TERMS, COEF_ROWS, 2 * PATCH_CELLS), jnp.bfloat16),
        ],
        cost_estimate=pl.CostEstimate(
            flops=2 * FIELDS * PATCH_CELLS * MEMBERS * MEMBERS * OWN_TERMS,
            bytes_accessed=FIELDS * MEMBERS * PATCH_CELLS * 8,
            transcendentals=0,
        ),
        compiler_params=pltpu.CompilerParams(vmem_limit_bytes=16 * MIB),
        name="own_part",
    )(message, coefs, background)


def lat_weights():
    lat = lax.axis_index("lat")
    lat_par = lat & 1
    lane = lax.broadcasted_iota(jnp.int32, (COEF_ROWS, PATCH_CELLS), 1)
    group = lane >> 5
    last = (lane & 1) == 1
    before = jnp.logical_and(last, (lane & (CELLS_LAT - 1)) != CELLS_LAT - 1)
    col = jnp.where(before, (group + CELLS_LON - 1) & (CELLS_LON - 1), group)
    weights = []
    for which in range(2):
        edge = jnp.where(lat_par == which, 1, 0)
        inside = jnp.where(lat_par == which, lat < N_LAT - 1, lat > 0)
        quarter = jnp.where(inside, 0.25, 0.0)
        for region in (0, 1, -1, LON_PAIRS):
            weight = jnp.where((lane & 1) == edge, quarter * lon_weight(col, region), 0.0)
            weights.append(weight.astype(jnp.bfloat16))
    return weights


def lat_kernel(lat_a_ref, lat_b_ref, right_ref, sum_ref, final_ref, left_ref, out_ref, sems):
    for which, ref in enumerate((lat_a_ref, lat_b_ref)):
        for tile in range(2):
            at = (2 * which + tile) * 128
            left_ref[:, at : at + 128] = ref[tile * MEMBERS : (tile + 1) * MEMBERS, :]
    parts = []
    for tile in range(LAT_TILES):
        parts.append(
            lax.dot_general(
                left_ref[...],
                right_ref[tile],
                (((1,), (0,)), ((), ())),
                preferred_element_type=jnp.float32,
            )
        )
    edges = lat_lanes(0)
    copies = []
    for first in range(0, FIELDS, CHUNK):
        stop = min(first + CHUNK, FIELDS)
        for field in range(first, stop):
            shift = 2 * (field % LAT_GROUP)
            part = parts[field // LAT_GROUP]
            moved = pltpu.roll(part, PATCH_CELLS - shift, 1) if shift else part
            out_ref[field] = (sum_ref[field] + jnp.where(edges, moved, 0.0)).astype(jnp.bfloat16)
        span = pl.ds(first, stop - first)
        copy = pltpu.make_async_copy(out_ref.at[span], final_ref.at[span], sems.at[first // CHUNK])
        copy.start()
        copies.append(copy)
    for copy in copies:
        copy.wait()


def lat_part(lat_a, lat_b, right, sums):
    return pl.pallas_call(
        lat_kernel,
        out_shape=jax.ShapeDtypeStruct(sums.shape, jnp.bfloat16),
        in_specs=[VMEM] * 4,
        out_specs=pl.BlockSpec(memory_space=pl.ANY),
        scratch_shapes=[
            pltpu.VMEM((MEMBERS, LAT_TERMS * MEMBERS), jnp.bfloat16),
            pltpu.VMEM((FIELDS, MEMBERS, PATCH_CELLS), jnp.bfloat16),
            pltpu.SemaphoreType.DMA(((FIELDS + CHUNK - 1) // CHUNK,)),
        ],
        compiler_params=pltpu.CompilerParams(vmem_limit_bytes=16 * MIB),
        name="lat_part",
    )(lat_a, lat_b, right, sums)


def side_kernel(
    core_ref, swap_ref, edge_ref, rows_ref, sum_ref, out_ref, right_ref, left_ref, weight_ref
):
    f32 = jnp.float32
    bf16 = jnp.bfloat16
    lon_par = lax.axis_index("lon") & 1
    col = cell_lanes(COEF_ROWS)[0]
    for source, ref in enumerate((core_ref, swap_ref)):
        for tile in range(3):
            at = (source * 3 + tile) * 128
            left_ref[:, at : at + 128] = ref[tile * MEMBERS : (tile + 1) * MEMBERS, :]
        mine = col == jnp.where(lon_par == source, CELLS_LON - 1, 0)
        coefs = jnp.where(mine, ref[PAIR_ROWS + MEMBERS :, :].astype(f32), 0.0)
        coefs = coefs + pltpu.roll(coefs, PATCH_CELLS // 2, 1)
        for k in range(6):
            weight_ref[source * 6 + k] = spread(coefs[k : k + 1], 2 * PATCH_CELLS).astype(bf16)
    for k, weight in enumerate(lat_weights()):
        weight = jnp.concatenate([weight] * (MEMBERS // COEF_ROWS), axis=0)
        for tile in range(LAT_TILES):
            right_ref[tile, pl.ds(k * MEMBERS, MEMBERS), :] = rows_ref[tile] * weight
    outer = side_lanes()

    def group(first, count):
        tiles = (count + 1) // 2
        edges = [edge_ref[first // 2 + t] for t in range(tiles)]
        both = jnp.concatenate(edges, axis=1) if tiles == 2 else edges[0]
        total = weighted_product(left_ref, weight_ref, SIDE_TERMS, both)
        for f in range(count):
            piece = total[:, f // 2 * PATCH_CELLS : (f // 2 + 1) * PATCH_CELLS]
            if f % 2:
                piece = pltpu.roll(piece, PATCH_CELLS // 2, 1)
            out_ref[first + f] = sum_ref[first + f] + jnp.where(outer, piece, 0.0)

    for first in range(0, FIELDS, 4):
        group(first, min(4, FIELDS - first))


def side_part(from_core, from_swap, edges, rows, sums):
    bf16 = jnp.bfloat16
    return pl.pallas_call(
        side_kernel,
        out_shape=(
            jax.ShapeDtypeStruct(sums.shape, sums.dtype),
            jax.ShapeDtypeStruct((LAT_TILES, LAT_TERMS * MEMBERS, PATCH_CELLS), bf16),
        ),
        in_specs=[VMEM] * 5,
        out_specs=(VMEM, VMEM),
        scratch_shapes=[
            pltpu.VMEM((MEMBERS, SIDE_TERMS * MEMBERS), bf16),
            pltpu.VMEM((SIDE_TERMS, COEF_ROWS, 2 * PATCH_CELLS), bf16),
        ],
        cost_estimate=pl.CostEstimate(
            flops=FIELDS * PATCH_CELLS * MEMBERS * MEMBERS * SIDE_TERMS,
            bytes_accessed=FIELDS * MEMBERS * PATCH_CELLS * 7,
            transcendentals=0,
        ),
        compiler_params=pltpu.CompilerParams(vmem_limit_bytes=16 * MIB),
        name="side_part",
    )(from_core, from_swap, edges, rows, sums)


CORES = [(i, i ^ 1) for i in range(32)]


def chip_transforms(
    depth, both, obs_ens, obs_value, obs_prec, slot_owner, info, counts, region_slots
):
    if depth > 1:
        rest = tuple(range(1, depth))
        send, keep, held, _, _ = split_of(rest, slot_owner, obs_ens, obs_value, obs_prec)
        got = lax.ppermute(send, "lon", CORES)
        both = merge_of(held, keep, got, both)
    received = lax.all_to_all(both, "lon", 0, 0, axis_index_groups=SAME_CORE, tiled=True)
    blocks = received.reshape(CHIPS * depth, ROWS, OBS_BLOCK)
    return transforms_of(depth, info, counts, region_slots, blocks)


def shards(background, obs_ens, obs_value, obs_prec, obs_count, slot_owner, region_slots):
    send, keep, held, info, index = split_of((0,), slot_owner, obs_ens, obs_value, obs_prec)
    got = lax.ppermute(send, "lon", CORES)
    both = merge_of(held, keep, got)
    operands = (
        both,
        obs_ens,
        obs_value,
        obs_prec,
        slot_owner,
        info,
        obs_count[:, 0, 0],
        jnp.transpose(region_slots, (0, 2, 1)),
    )
    branches = [functools.partial(chip_transforms, depth) for depth in (1, 2, SLOTS)]
    to_core, to_swap, edge_a, edge_b, coefs = lax.switch(
        index[0, 0], branches, *operands
    )

    swap = [(i, (i + 1) % 32) for i in range(1, 32, 2)] + [((i + 1) % 32, i) for i in range(1, 32, 2)]
    from_core = lax.ppermute(to_core, "lon", CORES)
    from_swap = lax.ppermute(to_swap, "lon", swap)
    state = background.reshape(FIELDS, MEMBERS, PATCH_CELLS)
    sums, edges, rows = own_part(to_core, coefs, state)
    message_a, message_b = pack_of(edge_a, edge_b, from_core, from_swap)
    pairs_a = [(i, i ^ 1) for i in range(8)]
    pairs_b = []
    for i in range(N_LAT):
        for j in range(32):
            if i in (0, N_LAT - 1):
                target = i * 32 + (j ^ 1)
            else:
                target = (i + 1 if i % 2 else i - 1) * 32 + j
            pairs_b.append((i * 32 + j, target))
    lat_b = lax.ppermute(message_b, ("lat", "lon"), pairs_b)
    lat_a = lax.ppermute(message_a, "lat", pairs_a)
    sums, right = side_part(from_core, from_swap, edges, rows, sums)
    result = lat_part(lat_a, lat_b, right, sums)
    return result.reshape(FIELDS, MEMBERS, 1, 1, PATCH_CELLS)


def solution(mesh):
    in_specs = (
        P(None, None, "lon", "lat", None),
        P(None, "lat", "lon", None, None, None),
        P(None, "lat", "lon", None, None),
        P(None, "lat", "lon", None, None),
        P(None, "lat", "lon"),
        P(),
        P("lon", "lat", None),
    )
    out_specs = P(None, None, "lon", "lat", None)
    return jax.shard_map(shards, mesh=mesh, in_specs=in_specs, out_specs=out_specs, check_vma=False)
```

profile of v0, /device:TPU:6, one launch (start us, length us, event | category | flops | bytes accessed | tf_op | source)
XLA Modules:
  0.0 47.5 jit_solution(10502464379713818227)
XLA Ops:
  0.0 0.0 copy-start.1
  0.0 0.0 copy-start.2
  0.0 0.0 copy-start.3
  0.0 0.0 copy-start.4
  0.0 0.0 copy-start.5
  0.0 0.0 copy-start.6
  0.0 1.9 %split.5 = (bf16[16,1,66,128]{3,2,1,0:T(8,128)(2,1)S(1)}, bf16[16,1,66,128]{3,2,1,0:T(8,128)(2,1)S(1)}, f32[1,16,128]{2,1,0:T(8,128)S(1)}, f32[8,128]{1,0:T(8,128)S(1)}, s32[8,128]{1,0:T(8,128)S(1)}) custom-call(s32[4]{0:T(128)} %owner_ref.1, bf16[4,16,2,64,128]{4,3,2,1,0:T(8,128)(2,1)} %bitcast.37, bf16[4,32,128]{2,1,0:T(8,128)(2,1)} %bitcast.40, ...), custom_call_target="tpu_custom_call" | custom-call | tf_op jit(solution)/shard_map/split/pallas_call | solution.py:143
  2.0 0.1 collective-permute-start.2
  2.1 0.5 %slice.3 = s32[1,1]{1,0:T(1,128)} slice(s32[8,128]{1,0:T(8,128)S(1)} %get-tuple-element.88), slice={[0:1], [0:1]} | slice | bytes 8 | tf_op jit(solution)/shard_map/slice | solution.py:637
  3.2 0.4 collective-permute-done.2.got_ref
  3.6 0.1 merge.5
  3.7 0.0 copy-done.1
  3.7 0.0 copy-done.2
  3.7 0.0 copy-done.3
  3.7 0.0 copy-done.4
  3.7 0.0 copy-done.5
  3.8 0.0 copy-done.6
  3.8 0.0 copy-start
  3.8 27.3 %conditional.1 = ((bf16[272,128]{1,0:T(8,128)(2,1)S(1)}, bf16[272,128]{1,0:T(8,128)(2,1)S(1)}, bf16[64,128]{1,0:T(8,128)(2,1)S(1)}, bf16[64,128]{1,0:T(8,128)(2,1)S(1)}, bf16[16,128]{1,0:T(8,128)(2,1)S(1)})) conditional(s32[]{:T(128)} %bitcast.27, (s32[4,1,1]{0,2,1:T(1,128)S(1)}, bf16[16,1,66,128]{3,2,1,0:T(8,128)(2,1)S(1)}, ...), branch_computations={%region_0.0_spmd, %region_1.0_spmd, %region_2.0_spmd} | conditional | bytes 12976176 | solution.py:636
  3.8 25.5 %all_to_all.12 = bf16[16,1,66,128]{3,2,1,0:T(8,128)(2,1)S(1)} all-to-all(bf16[16,1,66,128]{3,2,1,0:T(8,128)(2,1)S(1)} %get-tuple-element.48), channel_id=1, replica_groups={{0,2,4,6,8,10,12,14,16,18,20,22,24,26,28,30},{1,3,5,7,9,11,13,15,17,19,..., dimensions={0} | all-to-all | bytes 540672 | tf_op jit(solution)/shard_map/cond/branch_0_fun/all_to_all | solution.py:616
  29.3 1.8 %transforms.3 = (bf16[272,128]{1,0:T(8,128)(2,1)S(1)}, bf16[272,128]{1,0:T(8,128)(2,1)S(1)}, bf16[64,128]{1,0:T(8,128)(2,1)S(1)}, bf16[64,128]{1,0:T(8,128)(2,1)S(1)}, bf16[16,128]{1,0:T(8,128)(2,1)S(1)}) custom-call(f32[8,128]{1,0:T(8,128)S(1)} %get-tuple-element.45.info_ref, s32[1,4]{1,0:T(1,128)S(1)} %bitcast.49, ...), custom_call_target="tpu_custom_call" | custom-call | tf_op jit(solution)/shard_map/cond/branch_0_fun/transforms/pallas_call | solution.py:329
  31.1 0.1 collective-permute-start.3
  31.2 0.3 collective-permute-start.4
  31.5 0.0 copy-done
  31.5 1.7 %own_part.1 = (f32[69,64,128]{2,1,0:T(8,128)S(1)}, bf16[35,64,128]{2,1,0:T(8,128)(2,1)S(1)}, bf16[5,64,128]{2,1,0:T(8,128)(2,1)S(1)}) custom-call(bf16[272,128]{1,0:T(8,128)(2,1)S(1)} %get-tuple-element.95.pair_ref, bf16[16,128]{1,0:T(8,128)(2,1)S(1)} %get-tuple-element.99.coef_ref, bf16[69,64,128]{2,1,0:T(8,128)(2,1)S(1)} %bitcast.36), custom_call_target="tpu_custom_call" | custom-call | flops 434110464 | bytes 4521984 | tf_op jit(solution)/shard_map/own_part/pallas_call | solution.py:454
  33.2 0.0 collective-permute-done.3.core_ref
  33.2 5.6 %collective-permute-done.4.swap_ref = bf16[272,128]{1,0:T(8,128)(2,1)S(1)} collective-permute-done((bf16[272,128]{1,0:T(8,128)(2,1)S(1)}, bf16[272,128]{1,0:T(8,128)(2,1)S(1)}, u32[]{:S(2)}, u32[]{:S(2)}) %collective-permute-start.4) | collective-permute-done | bytes 69664 | tf_op jit(solution)/shard_map/ppermute | solution.py:642
  38.8 0.1 pack.1
  38.9 0.9 %collective-permute-start.5 = (bf16[128,128]{1,0:T(8,128)(2,1)S(1)}, bf16[128,128]{1,0:T(8,128)(2,1)S(1)}, u32[]{:S(2)}, u32[]{:S(2)}) collective-permute-start(bf16[128,128]{1,0:T(8,128)(2,1)S(1)} %get-tuple-element.97), channel_id=1, source_target_pairs={{0,32},{32,0},{64,96},{96,64},{128,160},{160,128},{192,224},{224,1... | collective-permute-start | bytes 98312 | tf_op jit(solution)/shard_map/ppermute | solution.py:656
  39.8 1.3 %collective-permute-start.6 = (bf16[128,128]{1,0:T(8,128)(2,1)S(1)}, bf16[128,128]{1,0:T(8,128)(2,1)S(1)}, u32[]{:S(2)}, u32[]{:S(2)}) collective-permute-start(bf16[128,128]{1,0:T(8,128)(2,1)S(1)} %get-tuple-element.98), channel_id=1, source_target_pairs={{0,1},{1,0},{2,3},{3,2},{4,5},{5,4},{6,7},{7,6},{8,9},{9,8},{10,11... | collective-permute-start | bytes 98312 | tf_op jit(solution)/shard_map/ppermute | solution.py:655
  41.1 1.3 %side_part.1 = (f32[69,64,128]{2,1,0:T(8,128)S(1)}, bf16[5,512,128]{2,1,0:T(8,128)(2,1)S(1)}) custom-call(bf16[272,128]{1,0:T(8,128)(2,1)S(1)} %collective-permute-done.3.core_ref, bf16[272,128]{1,0:T(8,128)(2,1)S(1)} %collective-permute-done.4.swap_ref, bf16[35,64,128]{2,1,0:T(8,128)(2,1)S(1)} %get-tuple-element.100.edge_ref, ...), custom_call_target="tpu_custom_call" | custom-call | flops 434110464 | bytes 3956736 | tf_op jit(solution)/shard_map/side_part/pallas_call | solution.py:583
  42.4 0.5 %collective-permute-done.5.lat_a_ref = bf16[128,128]{1,0:T(8,128)(2,1)S(1)} collective-permute-done((bf16[128,128]{1,0:T(8,128)(2,1)S(1)}, bf16[128,128]{1,0:T(8,128)(2,1)S(1)}, u32[]{:S(2)}, u32[]{:S(2)}) %collective-permute-start.5) | collective-permute-done | bytes 32800 | tf_op jit(solution)/shard_map/ppermute | solution.py:656
  42.9 2.9 %collective-permute-done.6.lat_b_ref = bf16[128,128]{1,0:T(8,128)(2,1)S(1)} collective-permute-done((bf16[128,128]{1,0:T(8,128)(2,1)S(1)}, bf16[128,128]{1,0:T(8,128)(2,1)S(1)}, u32[]{:S(2)}, u32[]{:S(2)}) %collective-permute-start.6) | collective-permute-done | bytes 32800 | tf_op jit(solution)/shard_map/ppermute | solution.py:655
  45.8 1.5 %lat_part.1 = bf16[69,64,128]{2,1,0:T(8,128)(2,1)} custom-call(bf16[128,128]{1,0:T(8,128)(2,1)S(1)} %collective-permute-done.5.lat_a_ref, bf16[128,128]{1,0:T(8,128)(2,1)S(1)} %collective-permute-done.6.lat_b_ref, bf16[5,512,128]{2,1,0:T(8,128)(2,1)S(1)} %get-tuple-element.103.right_ref, f32[69,64,128]{2,1,0:T(8,128)S(1)} %get-tuple-element.104.sum_ref), custom_call_target="tpu_custom_call" | custom-call | tf_op jit(solution)/shard_map/lat_part/pallas_call | solution.py:529
Async XLA Ops:
  0.0 3.7 %copy-start.1 = (bf16[4,1,1,32,64,128]{5,4,3,2,1,0:T(8,128)(2,1)S(1)}, bf16[4,1,1,32,64,128]{5,4,3,2,1,0:T(8,128)(2,1)}, u32[]{:S(2)}) copy-start(bf16[4,1,1,32,64,128]{5,4,3,2,1,0:T(8,128)(2,1)} %param.11) | copy-start | bytes 6291460
  0.0 3.7 %copy-start.2 = (bf16[4,1,1,32,128]{4,3,2,1,0:T(8,128)(2,1)S(1)}, bf16[4,1,1,32,128]{4,3,2,1,0:T(8,128)(2,1)}, u32[]{:S(2)}) copy-start(bf16[4,1,1,32,128]{4,3,2,1,0:T(8,128)(2,1)} %param.12) | copy-start | bytes 98308
  0.0 3.7 %copy-start.3 = (bf16[4,1,1,32,128]{4,3,2,1,0:T(8,128)(2,1)S(1)}, bf16[4,1,1,32,128]{4,3,2,1,0:T(8,128)(2,1)}, u32[]{:S(2)}) copy-start(bf16[4,1,1,32,128]{4,3,2,1,0:T(8,128)(2,1)} %param.13) | copy-start | bytes 98308
  0.0 3.7 %copy-start.4 = (s32[2,16,2]{1,2,0:T(2,128)S(1)}, s32[2,16,2]{1,2,0:T(2,128)}, u32[]{:S(2)}) copy-start(s32[2,16,2]{1,2,0:T(2,128)} %param.16) | copy-start | bytes 772
  0.0 3.7 %copy-start.5 = (s32[4]{0:T(128)S(1)}, s32[4]{0:T(128)}, u32[]{:S(2)}) copy-start(s32[4]{0:T(128)} %owner_ref.1) | copy-start | bytes 52
  0.0 3.7 %copy-start.6 = (s32[4,1,1]{0,2,1:T(1,128)S(1)}, s32[4,1,1]{0,2,1:T(1,128)}, u32[]{:S(2)}) copy-start(s32[4,1,1]{0,2,1:T(1,128)} %param.14) | copy-start | bytes 52
  2.0 1.7 %collective-permute-start.2 = (bf16[16,1,66,128]{3,2,1,0:T(8,128)(2,1)S(1)}, bf16[16,1,66,128]{3,2,1,0:T(8,128)(2,1)S(1)}, u32[]{:S(2)}, u32[]{:S(2)}) collective-permute-start(bf16[16,1,66,128]{3,2,1,0:T(8,128)(2,1)S(1)} %get-tuple-element.91), channel_id=1, source_target_pairs={{0,1},{1,0},{2,3},{3,2},{4,5},{5,4},{6,7},{7,6},{8,9},{9,8},{10,11... | collective-permute-start | bytes 811016 | tf_op jit(solution)/shard_map/ppermute | solution.py:623
  3.8 27.7 %copy-start = (bf16[69,64,1,1,128]{4,1,3,2,0:T(8,128)(2,1)S(1)}, bf16[69,64,1,1,128]{4,1,3,2,0:T(8,128)(2,1)}, u32[]{:S(2)}) copy-start(bf16[69,64,1,1,128]{4,1,3,2,0:T(8,128)(2,1)} %param.10) | copy-start | bytes 3391492
  31.1 2.1 %collective-permute-start.3 = (bf16[272,128]{1,0:T(8,128)(2,1)S(1)}, bf16[272,128]{1,0:T(8,128)(2,1)S(1)}, u32[]{:S(2)}, u32[]{:S(2)}) collective-permute-start(bf16[272,128]{1,0:T(8,128)(2,1)S(1)} %get-tuple-element.95.pair_ref), channel_id=1, source_target_pairs={{0,1},{1,0},{2,3},{3,2},{4,5},{5,4},{6,7},{7,6},{8,9},{9,8},{10,11... | collective-permute-start | bytes 208904 | tf_op jit(solution)/shard_map/ppermute | solution.py:641
  31.2 7.6 %collective-permute-start.4 = (bf16[272,128]{1,0:T(8,128)(2,1)S(1)}, bf16[272,128]{1,0:T(8,128)(2,1)S(1)}, u32[]{:S(2)}, u32[]{:S(2)}) collective-permute-start(bf16[272,128]{1,0:T(8,128)(2,1)S(1)} %get-tuple-element.96), channel_id=1, source_target_pairs={{1,2},{3,4},{5,6},{7,8},{9,10},{11,12},{13,14},{15,16},{17,18},{19... | collective-permute-start | bytes 208904 | tf_op jit(solution)/shard_map/ppermute | solution.py:642
  38.9 4.0 %collective-permute-start.5 = (bf16[128,128]{1,0:T(8,128)(2,1)S(1)}, bf16[128,128]{1,0:T(8,128)(2,1)S(1)}, u32[]{:S(2)}, u32[]{:S(2)}) collective-permute-start(bf16[128,128]{1,0:T(8,128)(2,1)S(1)} %get-tuple-element.97), channel_id=1, source_target_pairs={{0,32},{32,0},{64,96},{96,64},{128,160},{160,128},{192,224},{224,1... | collective-permute-start | bytes 98312 | tf_op jit(solution)/shard_map/ppermute | solution.py:656
  39.8 6.0 %collective-permute-start.6 = (bf16[128,128]{1,0:T(8,128)(2,1)S(1)}, bf16[128,128]{1,0:T(8,128)(2,1)S(1)}, u32[]{:S(2)}, u32[]{:S(2)}) collective-permute-start(bf16[128,128]{1,0:T(8,128)(2,1)S(1)} %get-tuple-element.98), channel_id=1, source_target_pairs={{0,1},{1,0},{2,3},{3,2},{4,5},{5,4},{6,7},{7,6},{8,9},{9,8},{10,11... | collective-permute-start | bytes 98312 | tf_op jit(solution)/shard_map/ppermute | solution.py:655
where the time goes:
time: 47.7 us; the launch traced here: 47.5 us
  blocking collectives  25.5 us (53%)
  waiting for transfers between devices  9.5 us (20%)
  Pallas kernels  8.32 us (17%)
  starting transfers between devices  2.62 us (5%)
  between operations  0.97 us (2%)
  local copies, waits for them, and re-layouts  0.54 us (1%)
    all_to_all x1, blocking collectives, chip_transforms(): lax.all_to_all(both, 'lon', 0, 0, axis_index_groups=SAME_CORE, tiled=True)  25.5 us
    ppermute x1, waiting for transfers between devices, shards(): from_swap = lax.ppermute(to_swap, 'lon', swap)  5.65 us
    ppermute x1, waiting for transfers between devices, shards(): lat_b = lax.ppermute(message_b, ('lat', 'lon'), pairs_b)  2.94 us
    pallas_call x1, Pallas kernels, split_of(): pl.pallas_call(functools.partial(split_kernel, places), out_shape=(shape,...  1.91 us
    pallas_call x1, Pallas kernels, transforms_of(): pl.pallas_call(functools.partial(transform_kernel, depth), out_shape=(mes...  1.76 us
    pallas_call x1, Pallas kernels, own_part(): pl.pallas_call(own_kernel, out_shape=(tiles(FIELDS, jnp.float32), tiles(H...  1.66 us
    pallas_call x1, Pallas kernels, lat_part(): pl.pallas_call(lat_kernel, out_shape=jax.ShapeDtypeStruct(sums.shape, jnp...  1.52 us
    pallas_call x1, Pallas kernels, side_part(): pl.pallas_call(side_kernel, out_shape=(jax.ShapeDtypeStruct(sums.shape, s...  1.31 us
  transfers between devices with their start and end apart: 5, of which 4 were waited for; matrix products, arithmetic and copies ran while one was open for 1% of the time, Pallas kernels for 6%

commit v1 on v0

--- a/solution.py
+++ b/solution.py
@@ -125,8 +125,8 @@
     for copy in smalls:
         copy.wait()
     for q in range(len(places)):
-        rows_ref[0] = small_ref[2 * q].astype(f32)
-        rows_ref[1] = small_ref[2 * q + 1].astype(f32)
+        rows_ref[0, 0 : 2 * CHIPS] = small_ref[2 * q].astype(f32)
+        rows_ref[1, 0 : 2 * CHIPS] = small_ref[2 * q + 1].astype(f32)
         for ref, side in targets:
             value = rows_ref[0, pl.ds(side, CHIPS, stride=2), :]
             prec = rows_ref[1, pl.ds(side, CHIPS, stride=2), :]
@@ -152,7 +152,7 @@
         in_specs=[SMEM] + [pl.BlockSpec(memory_space=pl.ANY)] * 3,
         out_specs=(VMEM,) * 5,
         scratch_shapes=[
-            pltpu.VMEM((2, 2 * CHIPS, OBS_BLOCK), jnp.float32),
+            pltpu.VMEM((2, 2 * CHIPS + 8, OBS_BLOCK), jnp.float32),
             pltpu.VMEM((2 * count, 2 * CHIPS, OBS_BLOCK), jnp.bfloat16),
             pltpu.SemaphoreType.DMA((2 * count,)),
             pltpu.SemaphoreType.DMA((2 * count,)),

time: 47.7 us -> 47.7 us (level)
  no operation moved by 1% of the time
where the time goes in v1:
time: 47.7 us; the launch traced here: 47.5 us
  blocking collectives  25.5 us (53%)
  waiting for transfers between devices  9.5 us (20%)
  Pallas kernels  8.32 us (17%)
  starting transfers between devices  2.62 us (5%)
  between operations  0.97 us (2%)
  local copies, waits for them, and re-layouts  0.54 us (1%)
    all_to_all x1, blocking collectives, chip_transforms(): lax.all_to_all(both, 'lon', 0, 0, axis_index_groups=SAME_CORE, tiled=True)  25.5 us
    ppermute x1, waiting for transfers between devices, shards(): from_swap = lax.ppermute(to_swap, 'lon', swap)  5.65 us
    ppermute x1, waiting for transfers between devices, shards(): lat_b = lax.ppermute(message_b, ('lat', 'lon'), pairs_b)  2.94 us
    pallas_call x1, Pallas kernels, split_of(): pl.pallas_call(functools.partial(split_kernel, places), out_shape=(shape,...  1.91 us
    pallas_call x1, Pallas kernels, transforms_of(): pl.pallas_call(functools.partial(transform_kernel, depth), out_shape=(mes...  1.76 us
    pallas_call x1, Pallas kernels, own_part(): pl.pallas_call(own_kernel, out_shape=(tiles(FIELDS, jnp.float32), tiles(H...  1.66 us
    pallas_call x1, Pallas kernels, lat_part(): pl.pallas_call(lat_kernel, out_shape=jax.ShapeDtypeStruct(sums.shape, jnp...  1.52 us
    pallas_call x1, Pallas kernels, side_part(): pl.pallas_call(side_kernel, out_shape=(jax.ShapeDtypeStruct(sums.shape, s...  1.31 us
  transfers between devices with their start and end apart: 5, of which 4 were waited for; matrix products, arithmetic and copies ran while one was open for 1% of the time, Pallas kernels for 6%

profile of v1, /device:TPU:6, one launch (start us, length us, event | category | flops | bytes accessed | tf_op | source)
XLA Modules:
  0.0 47.5 jit_solution(2423016461888053458)
XLA Ops:
  0.0 0.0 copy-start.1
  0.0 0.0 copy-start.2
  0.0 0.0 copy-start.3
  0.0 0.0 copy-start.4
  0.0 0.0 copy-start.5
  0.0 0.0 copy-start.6
  0.0 1.9 %split.5 = (bf16[16,1,66,128]{3,2,1,0:T(8,128)(2,1)S(1)}, bf16[16,1,66,128]{3,2,1,0:T(8,128)(2,1)S(1)}, f32[1,16,128]{2,1,0:T(8,128)S(1)}, f32[8,128]{1,0:T(8,128)S(1)}, s32[8,128]{1,0:T(8,128)S(1)}) custom-call(s32[4]{0:T(128)} %owner_ref.1, bf16[4,16,2,64,128]{4,3,2,1,0:T(8,128)(2,1)} %bitcast.37, bf16[4,32,128]{2,1,0:T(8,128)(2,1)} %bitcast.40, ...), custom_call_target="tpu_custom_call" | custom-call | tf_op jit(solution)/shard_map/split/pallas_call | solution.py:143
  2.0 0.1 collective-permute-start.2
  2.1 0.5 %slice.3 = s32[1,1]{1,0:T(1,128)} slice(s32[8,128]{1,0:T(8,128)S(1)} %get-tuple-element.88), slice={[0:1], [0:1]} | slice | bytes 8 | tf_op jit(solution)/shard_map/slice | solution.py:637
  3.2 0.4 collective-permute-done.2.got_ref
  3.6 0.1 merge.5
  3.7 0.0 copy-done.1
  3.7 0.0 copy-done.2
  3.7 0.0 copy-done.3
  3.7 0.0 copy-done.4
  3.7 0.0 copy-done.5
  3.8 0.0 copy-done.6
  3.8 0.0 copy-start
  3.8 27.3 %conditional.1 = ((bf16[272,128]{1,0:T(8,128)(2,1)S(1)}, bf16[272,128]{1,0:T(8,128)(2,1)S(1)}, bf16[64,128]{1,0:T(8,128)(2,1)S(1)}, bf16[64,128]{1,0:T(8,128)(2,1)S(1)}, bf16[16,128]{1,0:T(8,128)(2,1)S(1)})) conditional(s32[]{:T(128)} %bitcast.27, (s32[4,1,1]{0,2,1:T(1,128)S(1)}, bf16[16,1,66,128]{3,2,1,0:T(8,128)(2,1)S(1)}, ...), branch_computations={%region_0.0_spmd, %region_1.0_spmd, %region_2.0_spmd} | conditional | bytes 12976176 | solution.py:636
  3.8 25.5 %all_to_all.12 = bf16[16,1,66,128]{3,2,1,0:T(8,128)(2,1)S(1)} all-to-all(bf16[16,1,66,128]{3,2,1,0:T(8,128)(2,1)S(1)} %get-tuple-element.48), channel_id=1, replica_groups={{0,2,4,6,8,10,12,14,16,18,20,22,24,26,28,30},{1,3,5,7,9,11,13,15,17,19,..., dimensions={0} | all-to-all | bytes 540672 | tf_op jit(solution)/shard_map/cond/branch_0_fun/all_to_all | solution.py:616
  29.3 1.8 %transforms.3 = (bf16[272,128]{1,0:T(8,128)(2,1)S(1)}, bf16[272,128]{1,0:T(8,128)(2,1)S(1)}, bf16[64,128]{1,0:T(8,128)(2,1)S(1)}, bf16[64,128]{1,0:T(8,128)(2,1)S(1)}, bf16[16,128]{1,0:T(8,128)(2,1)S(1)}) custom-call(f32[8,128]{1,0:T(8,128)S(1)} %get-tuple-element.45.info_ref, s32[1,4]{1,0:T(1,128)S(1)} %bitcast.49, ...), custom_call_target="tpu_custom_call" | custom-call | tf_op jit(solution)/shard_map/cond/branch_0_fun/transforms/pallas_call | solution.py:329
  31.1 0.1 collective-permute-start.3
  31.2 0.3 collective-permute-start.4
  31.5 0.0 copy-done
  31.5 1.7 %own_part.1 = (f32[69,64,128]{2,1,0:T(8,128)S(1)}, bf16[35,64,128]{2,1,0:T(8,128)(2,1)S(1)}, bf16[5,64,128]{2,1,0:T(8,128)(2,1)S(1)}) custom-call(bf16[272,128]{1,0:T(8,128)(2,1)S(1)} %get-tuple-element.95.pair_ref, bf16[16,128]{1,0:T(8,128)(2,1)S(1)} %get-tuple-element.99.coef_ref, bf16[69,64,128]{2,1,0:T(8,128)(2,1)S(1)} %bitcast.36), custom_call_target="tpu_custom_call" | custom-call | flops 434110464 | bytes 4521984 | tf_op jit(solution)/shard_map/own_part/pallas_call | solution.py:454
  33.2 0.0 collective-permute-done.3.core_ref
  33.2 5.6 %collective-permute-done.4.swap_ref = bf16[272,128]{1,0:T(8,128)(2,1)S(1)} collective-permute-done((bf16[272,128]{1,0:T(8,128)(2,1)S(1)}, bf16[272,128]{1,0:T(8,128)(2,1)S(1)}, u32[]{:S(2)}, u32[]{:S(2)}) %collective-permute-start.4) | collective-permute-done | bytes 69664 | tf_op jit(solution)/shard_map/ppermute | solution.py:642
  38.8 0.1 pack.1
  38.9 0.9 %collective-permute-start.5 = (bf16[128,128]{1,0:T(8,128)(2,1)S(1)}, bf16[128,128]{1,0:T(8,128)(2,1)S(1)}, u32[]{:S(2)}, u32[]{:S(2)}) collective-permute-start(bf16[128,128]{1,0:T(8,128)(2,1)S(1)} %get-tuple-element.97), channel_id=1, source_target_pairs={{0,32},{32,0},{64,96},{96,64},{128,160},{160,128},{192,224},{224,1... | collective-permute-start | bytes 98312 | tf_op jit(solution)/shard_map/ppermute | solution.py:656
  39.8 1.3 %collective-permute-start.6 = (bf16[128,128]{1,0:T(8,128)(2,1)S(1)}, bf16[128,128]{1,0:T(8,128)(2,1)S(1)}, u32[]{:S(2)}, u32[]{:S(2)}) collective-permute-start(bf16[128,128]{1,0:T(8,128)(2,1)S(1)} %get-tuple-element.98), channel_id=1, source_target_pairs={{0,1},{1,0},{2,3},{3,2},{4,5},{5,4},{6,7},{7,6},{8,9},{9,8},{10,11... | collective-permute-start | bytes 98312 | tf_op jit(solution)/shard_map/ppermute | solution.py:655
  41.1 1.3 %side_part.1 = (f32[69,64,128]{2,1,0:T(8,128)S(1)}, bf16[5,512,128]{2,1,0:T(8,128)(2,1)S(1)}) custom-call(bf16[272,128]{1,0:T(8,128)(2,1)S(1)} %collective-permute-done.3.core_ref, bf16[272,128]{1,0:T(8,128)(2,1)S(1)} %collective-permute-done.4.swap_ref, bf16[35,64,128]{2,1,0:T(8,128)(2,1)S(1)} %get-tuple-element.100.edge_ref, ...), custom_call_target="tpu_custom_call" | custom-call | flops 434110464 | bytes 3956736 | tf_op jit(solution)/shard_map/side_part/pallas_call | solution.py:583
  42.4 0.5 %collective-permute-done.5.lat_a_ref = bf16[128,128]{1,0:T(8,128)(2,1)S(1)} collective-permute-done((bf16[128,128]{1,0:T(8,128)(2,1)S(1)}, bf16[128,128]{1,0:T(8,128)(2,1)S(1)}, u32[]{:S(2)}, u32[]{:S(2)}) %collective-permute-start.5) | collective-permute-done | bytes 32800 | tf_op jit(solution)/shard_map/ppermute | solution.py:656
  42.9 2.9 %collective-permute-done.6.lat_b_ref = bf16[128,128]{1,0:T(8,128)(2,1)S(1)} collective-permute-done((bf16[128,128]{1,0:T(8,128)(2,1)S(1)}, bf16[128,128]{1,0:T(8,128)(2,1)S(1)}, u32[]{:S(2)}, u32[]{:S(2)}) %collective-permute-start.6) | collective-permute-done | bytes 32800 | tf_op jit(solution)/shard_map/ppermute | solution.py:655
  45.8 1.5 %lat_part.1 = bf16[69,64,128]{2,1,0:T(8,128)(2,1)} custom-call(bf16[128,128]{1,0:T(8,128)(2,1)S(1)} %collective-permute-done.5.lat_a_ref, bf16[128,128]{1,0:T(8,128)(2,1)S(1)} %collective-permute-done.6.lat_b_ref, bf16[5,512,128]{2,1,0:T(8,128)(2,1)S(1)} %get-tuple-element.103.right_ref, f32[69,64,128]{2,1,0:T(8,128)S(1)} %get-tuple-element.104.sum_ref), custom_call_target="tpu_custom_call" | custom-call | tf_op jit(solution)/shard_map/lat_part/pallas_call | solution.py:529
Async XLA Ops:
  0.0 3.7 %copy-start.1 = (bf16[4,1,1,32,64,128]{5,4,3,2,1,0:T(8,128)(2,1)S(1)}, bf16[4,1,1,32,64,128]{5,4,3,2,1,0:T(8,128)(2,1)}, u32[]{:S(2)}) copy-start(bf16[4,1,1,32,64,128]{5,4,3,2,1,0:T(8,128)(2,1)} %param.11) | copy-start | bytes 6291460
  0.0 3.7 %copy-start.2 = (bf16[4,1,1,32,128]{4,3,2,1,0:T(8,128)(2,1)S(1)}, bf16[4,1,1,32,128]{4,3,2,1,0:T(8,128)(2,1)}, u32[]{:S(2)}) copy-start(bf16[4,1,1,32,128]{4,3,2,1,0:T(8,128)(2,1)} %param.12) | copy-start | bytes 98308
  0.0 3.7 %copy-start.3 = (bf16[4,1,1,32,128]{4,3,2,1,0:T(8,128)(2,1)S(1)}, bf16[4,1,1,32,128]{4,3,2,1,0:T(8,128)(2,1)}, u32[]{:S(2)}) copy-start(bf16[4,1,1,32,128]{4,3,2,1,0:T(8,128)(2,1)} %param.13) | copy-start | bytes 98308
  0.0 3.7 %copy-start.4 = (s32[2,16,2]{1,2,0:T(2,128)S(1)}, s32[2,16,2]{1,2,0:T(2,128)}, u32[]{:S(2)}) copy-start(s32[2,16,2]{1,2,0:T(2,128)} %param.16) | copy-start | bytes 772
  0.0 3.7 %copy-start.5 = (s32[4]{0:T(128)S(1)}, s32[4]{0:T(128)}, u32[]{:S(2)}) copy-start(s32[4]{0:T(128)} %owner_ref.1) | copy-start | bytes 52
  0.0 3.7 %copy-start.6 = (s32[4,1,1]{0,2,1:T(1,128)S(1)}, s32[4,1,1]{0,2,1:T(1,128)}, u32[]{:S(2)}) copy-start(s32[4,1,1]{0,2,1:T(1,128)} %param.14) | copy-start | bytes 52
  2.0 1.7 %collective-permute-start.2 = (bf16[16,1,66,128]{3,2,1,0:T(8,128)(2,1)S(1)}, bf16[16,1,66,128]{3,2,1,0:T(8,128)(2,1)S(1)}, u32[]{:S(2)}, u32[]{:S(2)}) collective-permute-start(bf16[16,1,66,128]{3,2,1,0:T(8,128)(2,1)S(1)} %get-tuple-element.91), channel_id=1, source_target_pairs={{0,1},{1,0},{2,3},{3,2},{4,5},{5,4},{6,7},{7,6},{8,9},{9,8},{10,11... | collective-permute-start | bytes 811016 | tf_op jit(solution)/shard_map/ppermute | solution.py:623
  3.8 27.7 %copy-start = (bf16[69,64,1,1,128]{4,1,3,2,0:T(8,128)(2,1)S(1)}, bf16[69,64,1,1,128]{4,1,3,2,0:T(8,128)(2,1)}, u32[]{:S(2)}) copy-start(bf16[69,64,1,1,128]{4,1,3,2,0:T(8,128)(2,1)} %param.10) | copy-start | bytes 3391492
  31.1 2.1 %collective-permute-start.3 = (bf16[272,128]{1,0:T(8,128)(2,1)S(1)}, bf16[272,128]{1,0:T(8,128)(2,1)S(1)}, u32[]{:S(2)}, u32[]{:S(2)}) collective-permute-start(bf16[272,128]{1,0:T(8,128)(2,1)S(1)} %get-tuple-element.95.pair_ref), channel_id=1, source_target_pairs={{0,1},{1,0},{2,3},{3,2},{4,5},{5,4},{6,7},{7,6},{8,9},{9,8},{10,11... | collective-permute-start | bytes 208904 | tf_op jit(solution)/shard_map/ppermute | solution.py:641
  31.2 7.6 %collective-permute-start.4 = (bf16[272,128]{1,0:T(8,128)(2,1)S(1)}, bf16[272,128]{1,0:T(8,128)(2,1)S(1)}, u32[]{:S(2)}, u32[]{:S(2)}) collective-permute-start(bf16[272,128]{1,0:T(8,128)(2,1)S(1)} %get-tuple-element.96), channel_id=1, source_target_pairs={{1,2},{3,4},{5,6},{7,8},{9,10},{11,12},{13,14},{15,16},{17,18},{19... | collective-permute-start | bytes 208904 | tf_op jit(solution)/shard_map/ppermute | solution.py:642
  38.9 4.0 %collective-permute-start.5 = (bf16[128,128]{1,0:T(8,128)(2,1)S(1)}, bf16[128,128]{1,0:T(8,128)(2,1)S(1)}, u32[]{:S(2)}, u32[]{:S(2)}) collective-permute-start(bf16[128,128]{1,0:T(8,128)(2,1)S(1)} %get-tuple-element.97), channel_id=1, source_target_pairs={{0,32},{32,0},{64,96},{96,64},{128,160},{160,128},{192,224},{224,1... | collective-permute-start | bytes 98312 | tf_op jit(solution)/shard_map/ppermute | solution.py:656
  39.8 6.0 %collective-permute-start.6 = (bf16[128,128]{1,0:T(8,128)(2,1)S(1)}, bf16[128,128]{1,0:T(8,128)(2,1)S(1)}, u32[]{:S(2)}, u32[]{:S(2)}) collective-permute-start(bf16[128,128]{1,0:T(8,128)(2,1)S(1)} %get-tuple-element.98), channel_id=1, source_target_pairs={{0,1},{1,0},{2,3},{3,2},{4,5},{5,4},{6,7},{7,6},{8,9},{9,8},{10,11... | collective-permute-start | bytes 98312 | tf_op jit(solution)/shard_map/ppermute | solution.py:655

commit v2 on v1

--- a/solution.py
+++ b/solution.py
@@ -336,8 +336,9 @@
     )(info, counts.reshape(1, SLOTS), region_slots, blocks)
 
 
-def pack_kernel(edge_a_ref, edge_b_ref, core_ref, swap_ref, out_a_ref, out_b_ref):
+def pack_kernel(which, edge_ref, core_ref, swap_ref, *refs):
     f32 = jnp.float32
+    out_ref = refs[-1]
     even = (lax.axis_index("lon") & 1) == 0
     first = lax.broadcasted_iota(jnp.int32, (MEMBERS, 2 * MEMBERS), 1) < MEMBERS
     rows = pl.ds(PAIR_ROWS, MEMBERS)
@@ -345,22 +346,26 @@
     swap = swap_ref[rows, :].astype(f32)
     before = jnp.where(even, swap, core)
     after = jnp.where(even, core, swap)
-    out_a_ref[0:MEMBERS] = edge_a_ref[...]
-    out_b_ref[0:MEMBERS] = edge_b_ref[...]
-    out_a_ref[MEMBERS:] = jnp.where(first, before, pltpu.roll(after, MEMBERS, 1)).astype(jnp.bfloat16)
-    out_b_ref[MEMBERS:] = jnp.where(first, pltpu.roll(before, MEMBERS, 1), after).astype(jnp.bfloat16)
-
-
-def pack_of(edge_a, edge_b, from_core, from_swap):
-    shape = jax.ShapeDtypeStruct((2 * MEMBERS, 2 * MEMBERS), jnp.bfloat16)
+    if which == 0:
+        after = pltpu.roll(after, MEMBERS, 1)
+    else:
+        before = pltpu.roll(before, MEMBERS, 1)
+    out_ref[0:MEMBERS] = edge_ref[...]
+    out_ref[MEMBERS:] = jnp.where(first, before, after).astype(jnp.bfloat16)
+
+
+def pack_of(which, edge, from_core, from_swap, *ahead):
     return pl.pallas_call(
-        pack_kernel,
-        out_shape=(shape, shape),
-        in_specs=[VMEM] * 4,
-        out_specs=(VMEM, VMEM),
+        functools.partial(pack_kernel, which),
+        out_shape=jax.ShapeDtypeStruct((2 * MEMBERS, 2 * MEMBERS), jnp.bfloat16),
+        in_specs=[VMEM] * (3 + len(ahead)),
+        out_specs=VMEM,
+        cost_estimate=pl.CostEstimate(
+            flops=1_000_000_000 * len(ahead), bytes_accessed=100_000, transcendentals=0
+        ),
         compiler_params=pltpu.CompilerParams(vmem_limit_bytes=4 * MIB),
         name="pack",
-    )(edge_a, edge_b, from_core, from_swap)
+    )(edge, from_core, from_swap, *ahead)
 
 
 def spread(row, width):
@@ -642,7 +647,8 @@
     from_swap = lax.ppermute(to_swap, "lon", swap)
     state = background.reshape(FIELDS, MEMBERS, PATCH_CELLS)
     sums, edges, rows = own_part(to_core, coefs, state)
-    message_a, message_b = pack_of(edge_a, edge_b, from_core, from_swap)
+    message_b = pack_of(1, edge_b, from_core, from_swap)
+    message_a = pack_of(0, edge_a, from_core, from_swap, message_b)
     pairs_a = [(i, i ^ 1) for i in range(8)]
     pairs_b = []
     for i in range(N_LAT):

time: 47.7 us -> 47.4 us (level); the launches traced: 47.5 us -> 46.6 us
  starting transfers between devices: 2.62 us -> 1.88 us
    ppermute x1, waiting for transfers between devices: 2.94 us -> 1.41 us  [shards(): lat_b = lax.ppermute(message_b, ('lat', 'lon'), pairs_b)]
    ppermute x1, waiting for transfers between devices: 0.51 us -> 1.82 us  [shards(): lat_a = lax.ppermute(message_a, 'lat', pairs_a)]
    ppermute x1, starting transfers between devices: 1.26 us -> 0.62 us  [shards(): lat_b = lax.ppermute(message_b, ('lat', 'lon'), pairs_b)]
  transfers between devices with their start and end apart: 5 -> 5, of which waited for: 4 -> 4; matrix products, arithmetic and copies ran while one was open for 1% -> 1% of each run, Pallas kernels for 6% -> 7%
where the time goes in v2:
time: 47.4 us; the launch traced here: 46.6 us
  blocking collectives  25.5 us (54%)
  waiting for transfers between devices  9.28 us (20%)
  Pallas kernels  8.4 us (18%)
  starting transfers between devices  1.88 us (4%)
  between operations  0.97 us (2%)
  local copies, waits for them, and re-layouts  0.54 us (1%)
    all_to_all x1, blocking collectives, chip_transforms(): lax.all_to_all(both, 'lon', 0, 0, axis_index_groups=SAME_CORE, tiled=True)  25.5 us
    ppermute x1, waiting for transfers between devices, shards(): from_swap = lax.ppermute(to_swap, 'lon', swap)  5.65 us
    pallas_call x1, Pallas kernels, split_of(): pl.pallas_call(functools.partial(split_kernel, places), out_shape=(shape,...  1.91 us
    ppermute x1, waiting for transfers between devices, shards(): lat_a = lax.ppermute(message_a, 'lat', pairs_a)  1.82 us
    pallas_call x1, Pallas kernels, transforms_of(): pl.pallas_call(functools.partial(transform_kernel, depth), out_shape=(mes...  1.76 us
    pallas_call x1, Pallas kernels, own_part(): pl.pallas_call(own_kernel, out_shape=(tiles(FIELDS, jnp.float32), tiles(H...  1.66 us
    pallas_call x1, Pallas kernels, lat_part(): pl.pallas_call(lat_kernel, out_shape=jax.ShapeDtypeStruct(sums.shape, jnp...  1.52 us
    ppermute x1, waiting for transfers between devices, shards(): lat_b = lax.ppermute(message_b, ('lat', 'lon'), pairs_b)  1.41 us
  transfers between devices with their start and end apart: 5, of which 4 were waited for; matrix products, arithmetic and copies ran while one was open for 1% of the time, Pallas kernels for 7%

profile of v2, /device:TPU:6, one launch (start us, length us, event | category | flops | bytes accessed | tf_op | source)
XLA Modules:
  0.0 46.6 jit_solution(4199260412168252265)
XLA Ops:
  0.0 0.0 copy-start.1
  0.0 0.0 copy-start.2
  0.0 0.0 copy-start.3
  0.0 0.0 copy-start.4
  0.0 0.0 copy-start.5
  0.0 0.0 copy-start.6
  0.0 1.9 %split.5 = (bf16[16,1,66,128]{3,2,1,0:T(8,128)(2,1)S(1)}, bf16[16,1,66,128]{3,2,1,0:T(8,128)(2,1)S(1)}, f32[1,16,128]{2,1,0:T(8,128)S(1)}, f32[8,128]{1,0:T(8,128)S(1)}, s32[8,128]{1,0:T(8,128)S(1)}) custom-call(s32[4]{0:T(128)} %owner_ref.1, bf16[4,16,2,64,128]{4,3,2,1,0:T(8,128)(2,1)} %bitcast.37, bf16[4,32,128]{2,1,0:T(8,128)(2,1)} %bitcast.40, ...), custom_call_target="tpu_custom_call" | custom-call | tf_op jit(solution)/shard_map/split/pallas_call | solution.py:143
  2.0 0.1 collective-permute-start.2
  2.1 0.5 %slice.3 = s32[1,1]{1,0:T(1,128)} slice(s32[8,128]{1,0:T(8,128)S(1)} %get-tuple-element.86), slice={[0:1], [0:1]} | slice | bytes 8 | tf_op jit(solution)/shard_map/slice | solution.py:642
  3.2 0.4 collective-permute-done.2.got_ref
  3.6 0.1 merge.5
  3.7 0.0 copy-done.1
  3.7 0.0 copy-done.2
  3.7 0.0 copy-done.3
  3.7 0.0 copy-done.4
  3.7 0.0 copy-done.5
  3.8 0.0 copy-done.6
  3.8 0.0 copy-start
  3.8 27.3 %conditional.1 = ((bf16[272,128]{1,0:T(8,128)(2,1)S(1)}, bf16[272,128]{1,0:T(8,128)(2,1)S(1)}, bf16[64,128]{1,0:T(8,128)(2,1)S(1)}, bf16[64,128]{1,0:T(8,128)(2,1)S(1)}, bf16[16,128]{1,0:T(8,128)(2,1)S(1)})) conditional(s32[]{:T(128)} %bitcast.27, (s32[4,1,1]{0,2,1:T(1,128)S(1)}, bf16[16,1,66,128]{3,2,1,0:T(8,128)(2,1)S(1)}, ...), branch_computations={%region_0.0_spmd, %region_1.0_spmd, %region_2.0_spmd} | conditional | bytes 12976176 | solution.py:641
  3.8 25.5 %all_to_all.12 = bf16[16,1,66,128]{3,2,1,0:T(8,128)(2,1)S(1)} all-to-all(bf16[16,1,66,128]{3,2,1,0:T(8,128)(2,1)S(1)} %get-tuple-element.48), channel_id=1, replica_groups={{0,2,4,6,8,10,12,14,16,18,20,22,24,26,28,30},{1,3,5,7,9,11,13,15,17,19,..., dimensions={0} | all-to-all | bytes 540672 | tf_op jit(solution)/shard_map/cond/branch_0_fun/all_to_all | solution.py:621
  29.3 1.8 %transforms.3 = (bf16[272,128]{1,0:T(8,128)(2,1)S(1)}, bf16[272,128]{1,0:T(8,128)(2,1)S(1)}, bf16[64,128]{1,0:T(8,128)(2,1)S(1)}, bf16[64,128]{1,0:T(8,128)(2,1)S(1)}, bf16[16,128]{1,0:T(8,128)(2,1)S(1)}) custom-call(f32[8,128]{1,0:T(8,128)S(1)} %get-tuple-element.45.info_ref, s32[1,4]{1,0:T(1,128)S(1)} %bitcast.49, ...), custom_call_target="tpu_custom_call" | custom-call | tf_op jit(solution)/shard_map/cond/branch_0_fun/transforms/pallas_call | solution.py:329
  31.1 0.1 collective-permute-start.3
  31.2 0.3 collective-permute-start.4
  31.5 0.0 copy-done
  31.5 1.7 %own_part.1 = (f32[69,64,128]{2,1,0:T(8,128)S(1)}, bf16[35,64,128]{2,1,0:T(8,128)(2,1)S(1)}, bf16[5,64,128]{2,1,0:T(8,128)(2,1)S(1)}) custom-call(bf16[272,128]{1,0:T(8,128)(2,1)S(1)} %get-tuple-element.92.pair_ref, bf16[16,128]{1,0:T(8,128)(2,1)S(1)} %get-tuple-element.95.coef_ref, bf16[69,64,128]{2,1,0:T(8,128)(2,1)S(1)} %bitcast.36), custom_call_target="tpu_custom_call" | custom-call | flops 434110464 | bytes 4521984 | tf_op jit(solution)/shard_map/own_part/pallas_call | solution.py:459
  33.2 0.0 collective-permute-done.3.core_ref
  33.2 5.6 %collective-permute-done.4.swap_ref = bf16[272,128]{1,0:T(8,128)(2,1)S(1)} collective-permute-done((bf16[272,128]{1,0:T(8,128)(2,1)S(1)}, bf16[272,128]{1,0:T(8,128)(2,1)S(1)}, u32[]{:S(2)}, u32[]{:S(2)}) %collective-permute-start.4) | collective-permute-done | bytes 69664 | tf_op jit(solution)/shard_map/ppermute | solution.py:647
  38.8 0.1 pack.2.refs_0_
  38.9 0.6 %collective-permute-start.6 = (bf16[128,128]{1,0:T(8,128)(2,1)S(1)}, bf16[128,128]{1,0:T(8,128)(2,1)S(1)}, u32[]{:S(2)}, u32[]{:S(2)}) collective-permute-start(bf16[128,128]{1,0:T(8,128)(2,1)S(1)} %pack.2.refs_0_), channel_id=1, source_target_pairs={{0,1},{1,0},{2,3},{3,2},{4,5},{5,4},{6,7},{7,6},{8,9},{9,8},{10,11... | collective-permute-start | bytes 98312 | tf_op jit(solution)/shard_map/ppermute | solution.py:661
  39.5 0.1 pack.3
  39.6 0.8 %collective-permute-start.5 = (bf16[128,128]{1,0:T(8,128)(2,1)S(1)}, bf16[128,128]{1,0:T(8,128)(2,1)S(1)}, u32[]{:S(2)}, u32[]{:S(2)}) collective-permute-start(bf16[128,128]{1,0:T(8,128)(2,1)S(1)} %pack.3), channel_id=1, source_target_pairs={{0,32},{32,0},{64,96},{96,64},{128,160},{160,128},{192,224},{224,1... | collective-permute-start | bytes 98312 | tf_op jit(solution)/shard_map/ppermute | solution.py:662
  40.4 1.3 %side_part.1 = (f32[69,64,128]{2,1,0:T(8,128)S(1)}, bf16[5,512,128]{2,1,0:T(8,128)(2,1)S(1)}) custom-call(bf16[272,128]{1,0:T(8,128)(2,1)S(1)} %collective-permute-done.3.core_ref, bf16[272,128]{1,0:T(8,128)(2,1)S(1)} %collective-permute-done.4.swap_ref, bf16[35,64,128]{2,1,0:T(8,128)(2,1)S(1)} %get-tuple-element.96.edge_ref, ...), custom_call_target="tpu_custom_call" | custom-call | flops 434110464 | bytes 3956736 | tf_op jit(solution)/shard_map/side_part/pallas_call | solution.py:588
  41.7 1.8 %collective-permute-done.5.lat_a_ref = bf16[128,128]{1,0:T(8,128)(2,1)S(1)} collective-permute-done((bf16[128,128]{1,0:T(8,128)(2,1)S(1)}, bf16[128,128]{1,0:T(8,128)(2,1)S(1)}, u32[]{:S(2)}, u32[]{:S(2)}) %collective-permute-start.5) | collective-permute-done | bytes 32800 | tf_op jit(solution)/shard_map/ppermute | solution.py:662
  43.5 1.4 %collective-permute-done.6.lat_b_ref = bf16[128,128]{1,0:T(8,128)(2,1)S(1)} collective-permute-done((bf16[128,128]{1,0:T(8,128)(2,1)S(1)}, bf16[128,128]{1,0:T(8,128)(2,1)S(1)}, u32[]{:S(2)}, u32[]{:S(2)}) %collective-permute-start.6) | collective-permute-done | bytes 32800 | tf_op jit(solution)/shard_map/ppermute | solution.py:661
  45.0 1.5 %lat_part.1 = bf16[69,64,128]{2,1,0:T(8,128)(2,1)} custom-call(bf16[128,128]{1,0:T(8,128)(2,1)S(1)} %collective-permute-done.5.lat_a_ref, bf16[128,128]{1,0:T(8,128)(2,1)S(1)} %collective-permute-done.6.lat_b_ref, bf16[5,512,128]{2,1,0:T(8,128)(2,1)S(1)} %get-tuple-element.99.right_ref, f32[69,64,128]{2,1,0:T(8,128)S(1)} %get-tuple-element.100.sum_ref), custom_call_target="tpu_custom_call" | custom-call | tf_op jit(solution)/shard_map/lat_part/pallas_call | solution.py:534
Async XLA Ops:
  0.0 3.7 %copy-start.1 = (bf16[4,1,1,32,64,128]{5,4,3,2,1,0:T(8,128)(2,1)S(1)}, bf16[4,1,1,32,64,128]{5,4,3,2,1,0:T(8,128)(2,1)}, u32[]{:S(2)}) copy-start(bf16[4,1,1,32,64,128]{5,4,3,2,1,0:T(8,128)(2,1)} %param.11) | copy-start | bytes 6291460
  0.0 3.7 %copy-start.2 = (bf16[4,1,1,32,128]{4,3,2,1,0:T(8,128)(2,1)S(1)}, bf16[4,1,1,32,128]{4,3,2,1,0:T(8,128)(2,1)}, u32[]{:S(2)}) copy-start(bf16[4,1,1,32,128]{4,3,2,1,0:T(8,128)(2,1)} %param.12) | copy-start | bytes 98308
  0.0 3.7 %copy-start.3 = (bf16[4,1,1,32,128]{4,3,2,1,0:T(8,128)(2,1)S(1)}, bf16[4,1,1,32,128]{4,3,2,1,0:T(8,128)(2,1)}, u32[]{:S(2)}) copy-start(bf16[4,1,1,32,128]{4,3,2,1,0:T(8,128)(2,1)} %param.13) | copy-start | bytes 98308
  0.0 3.7 %copy-start.4 = (s32[2,16,2]{1,2,0:T(2,128)S(1)}, s32[2,16,2]{1,2,0:T(2,128)}, u32[]{:S(2)}) copy-start(s32[2,16,2]{1,2,0:T(2,128)} %param.16) | copy-start | bytes 772
  0.0 3.7 %copy-start.5 = (s32[4]{0:T(128)S(1)}, s32[4]{0:T(128)}, u32[]{:S(2)}) copy-start(s32[4]{0:T(128)} %owner_ref.1) | copy-start | bytes 52
  0.0 3.7 %copy-start.6 = (s32[4,1,1]{0,2,1:T(1,128)S(1)}, s32[4,1,1]{0,2,1:T(1,128)}, u32[]{:S(2)}) copy-start(s32[4,1,1]{0,2,1:T(1,128)} %param.14) | copy-start | bytes 52
  2.0 1.7 %collective-permute-start.2 = (bf16[16,1,66,128]{3,2,1,0:T(8,128)(2,1)S(1)}, bf16[16,1,66,128]{3,2,1,0:T(8,128)(2,1)S(1)}, u32[]{:S(2)}, u32[]{:S(2)}) collective-permute-start(bf16[16,1,66,128]{3,2,1,0:T(8,128)(2,1)S(1)} %get-tuple-element.89), channel_id=1, source_target_pairs={{0,1},{1,0},{2,3},{3,2},{4,5},{5,4},{6,7},{7,6},{8,9},{9,8},{10,11... | collective-permute-start | bytes 811016 | tf_op jit(solution)/shard_map/ppermute | solution.py:628
  3.8 27.7 %copy-start = (bf16[69,64,1,1,128]{4,1,3,2,0:T(8,128)(2,1)S(1)}, bf16[69,64,1,1,128]{4,1,3,2,0:T(8,128)(2,1)}, u32[]{:S(2)}) copy-start(bf16[69,64,1,1,128]{4,1,3,2,0:T(8,128)(2,1)} %param.10) | copy-start | bytes 3391492
  31.1 2.1 %collective-permute-start.3 = (bf16[272,128]{1,0:T(8,128)(2,1)S(1)}, bf16[272,128]{1,0:T(8,128)(2,1)S(1)}, u32[]{:S(2)}, u32[]{:S(2)}) collective-permute-start(bf16[272,128]{1,0:T(8,128)(2,1)S(1)} %get-tuple-element.92.pair_ref), channel_id=1, source_target_pairs={{0,1},{1,0},{2,3},{3,2},{4,5},{5,4},{6,7},{7,6},{8,9},{9,8},{10,11... | collective-permute-start | bytes 208904 | tf_op jit(solution)/shard_map/ppermute | solution.py:646
  31.2 7.6 %collective-permute-start.4 = (bf16[272,128]{1,0:T(8,128)(2,1)S(1)}, bf16[272,128]{1,0:T(8,128)(2,1)S(1)}, u32[]{:S(2)}, u32[]{:S(2)}) collective-permute-start(bf16[272,128]{1,0:T(8,128)(2,1)S(1)} %get-tuple-element.93), channel_id=1, source_target_pairs={{1,2},{3,4},{5,6},{7,8},{9,10},{11,12},{13,14},{15,16},{17,18},{19... | collective-permute-start | bytes 208904 | tf_op jit(solution)/shard_map/ppermute | solution.py:647
  38.9 6.0 %collective-permute-start.6 = (bf16[128,128]{1,0:T(8,128)(2,1)S(1)}, bf16[128,128]{1,0:T(8,128)(2,1)S(1)}, u32[]{:S(2)}, u32[]{:S(2)}) collective-permute-start(bf16[128,128]{1,0:T(8,128)(2,1)S(1)} %pack.2.refs_0_), channel_id=1, source_target_pairs={{0,1},{1,0},{2,3},{3,2},{4,5},{5,4},{6,7},{7,6},{8,9},{9,8},{10,11... | collective-permute-start | bytes 98312 | tf_op jit(solution)/shard_map/ppermute | solution.py:661
  39.6 3.9 %collective-permute-start.5 = (bf16[128,128]{1,0:T(8,128)(2,1)S(1)}, bf16[128,128]{1,0:T(8,128)(2,1)S(1)}, u32[]{:S(2)}, u32[]{:S(2)}) collective-permute-start(bf16[128,128]{1,0:T(8,128)(2,1)S(1)} %pack.3), channel_id=1, source_target_pairs={{0,32},{32,0},{64,96},{96,64},{128,160},{160,128},{192,224},{224,1... | collective-permute-start | bytes 98312 | tf_op jit(solution)/shard_map/ppermute | solution.py:662
